TPU v7x, 256 devices: a whole 4x4x8 slice. The times are simulated.
256 devices in a mesh: row: 32 (over x, y, core), col: 8 (over z).
Axes of the slice: x: 4, y: 4, z: 8, core: 2. Of those that a mesh axis runs over, the one named last changes fastest.
Arguments:
- in_map: bfloat16 [512, 256, 256], P('row', 'col'), may hold values from -6 to 6
- tile_w: bfloat16 [3, 3, 256, 256], replicated, may hold values from -0.125 to 0.125
- head_w1: bfloat16 [3, 3, 256, 256], replicated, may hold values from -0.125 to 0.125
- head_w2: bfloat16 [3, 3, 256, 256], replicated, may hold values from -0.125 to 0.125
- box_row: int32 [512, 8], P('row', 'col'), may hold values from 0 to 2
- box_col: int32 [512, 8], P('row', 'col'), may hold values from 0 to 18
- box_target: int32 [512, 8], P('row', 'col'), may hold values from -1 to 31, as said below
- head_cot: bfloat16 [128, 8, 14, 14, 256], P('row', 'col'), may hold values from -6 to 6
Outputs:
- grad_map: bfloat16 [512, 256, 256], P('row', 'col')
- grad_w1: float32 [3, 3, 256, 256], replicated
- grad_w2: float32 [3, 3, 256, 256], replicated
Inputs may be any that keep to these rules, and one draw needn't show every extreme that they name: `box_target`: within each row r of tiles, every head slot d * 4 + h (d below 8, h below 4) is named by exactly one tile slot, and empty slots hold -1. A tile names at most 2 head slots of one device, so it holds at most 16 boxes; in every row of tiles one tile holds 16 boxes, 2 for each device of the row.
All inputs are finite; a program needn't handle non-finite values.
Results may differ from a plain program's by a relative error of at most 0.012.
Values may be sent and summed in bfloat16 or wider, within the bound.
A program may use at most 64 MiB of HBM per device.

v0:
```python
import math
import jax
import jax.numpy as jnp
from jax import lax
from jax.sharding import PartitionSpec as P

LAYOUT = ("NHWC", "HWIO", "NHWC")


def padded_2(shard, sides, width):
    for axis, dim in sides:
        size, length = (lax.axis_size(axis), shard.shape[dim])
        up = [(i, (i + 1) % size) for i in range(size - 1)]
        down = [(j, i) for i, j in up]
        last = lax.slice_in_dim(shard, length - width, length, axis=dim)
        leading = lax.slice_in_dim(shard, 0, width, axis=dim)
        before = lax.ppermute(last, axis, up)
        after = lax.ppermute(leading, axis, down)
        shard = jnp.concatenate([before, shard, after], axis=dim)
    return shard


def conv_pad(inputs, kernel, margin):
    return lax.conv_general_dilated(
        inputs,
        kernel,
        (1, 1),
        ((margin, margin), (margin, margin)),
        dimension_numbers=LAYOUT,
        preferred_element_type=jnp.float32,
    )


def flip_weights(kernel):
    return jnp.transpose(jnp.flip(kernel, (0, 1)), (0, 1, 3, 2))


def silu_slope(values):
    sigma = jax.nn.sigmoid(values)
    return sigma * (1.0 + values * (1.0 - sigma))


def weight_grad(inputs, deltas):
    channels = inputs.shape[-1]
    box_side = inputs.shape[1]
    padded = jnp.pad(inputs, ((0, 0), (1, 1), (1, 1), (0, 0)))
    flat_delta = deltas.reshape(-1, channels)
    blocks = []
    for shift_y in range(3):
        for shift_x in range(3):
            window = padded[
                :, shift_y : shift_y + box_side, shift_x : shift_x + box_side, :
            ].reshape(-1, channels)
            blocks.append(
                lax.dot_general(
                    window, flat_delta, (((0,), (0,)), ((), ())), preferred_element_type=jnp.float32
                )
            )
    return jnp.stack(blocks).reshape(3, 3, channels, channels)


def pick_rows(table, values):
    flat = values.reshape(values.shape[0], -1)
    return jnp.dot(table, flat, preferred_element_type=jnp.float32).astype(jnp.bfloat16)


def pick_back(table, values):
    return lax.dot_general(
        table, values, (((0,), (0,)), ((), ())), preferred_element_type=jnp.float32
    ).astype(jnp.bfloat16)


def body(in_map, tile_w, head_w1, head_w2, box_row, box_col, box_target, head_cot):
    tile_rows, tile_cols, channels = in_map.shape
    head_count = head_cot.shape[0]
    box_side = head_cot.shape[2]
    slot_count = box_target.shape[0]
    columns = lax.axis_size("col")
    capacity = slot_count // columns
    pair_count = columns * capacity
    padded = padded_2(in_map, (("row", 0), ("col", 1)), 1)
    preact = conv_pad(padded[None], tile_w, 0)[0]
    target = box_target[:, 0]
    occupied = target >= 0
    dest_col = jnp.where(occupied, target // head_count, 0)
    head_slot = jnp.where(occupied, target % head_count, 0)
    slot_ids = jnp.arange(slot_count, dtype=jnp.int32)
    same_dest = (dest_col[:, None] == dest_col[None, :]) & occupied[None, :]
    placing = jnp.sum(same_dest & (slot_ids[None, :] < slot_ids[:, None]), axis=1)
    pair_slot = dest_col * capacity + placing
    pair_ids = jnp.arange(pair_count, dtype=jnp.int32)
    send_map = ((pair_slot[None, :] == pair_ids[:, None]) & occupied[None, :]).astype(jnp.bfloat16)
    head_ids = jnp.arange(head_count, dtype=jnp.int32)
    head_hot = ((head_slot[:, None] == head_ids[None, :]) & occupied[:, None]).astype(jnp.bfloat16)
    pair_head = (
        jnp.dot(send_map, head_hot, preferred_element_type=jnp.float32)
        .astype(jnp.bfloat16)
        .reshape(columns, capacity, head_count)
    )
    top_row = box_row[:, 0]
    left_col = box_col[:, 0]
    zero_index = jnp.zeros((), jnp.int32)
    feature = jax.nn.silu(preact).astype(jnp.bfloat16)
    crops = jax.vmap(
        lambda y, x: lax.dynamic_slice(feature, (y, x, zero_index), (box_side, box_side, channels))
    )(top_row, left_col)
    outgoing = pick_rows(send_map, crops).reshape(columns, capacity, box_side, box_side, channels)
    arrived, arrived_head = (
        lax.all_to_all(outgoing, "col", split_axis=0, concat_axis=0, tiled=True),
        lax.all_to_all(pair_head, "col", split_axis=0, concat_axis=0, tiled=True),
    )
    arrived_head = arrived_head.reshape(pair_count, head_count)
    box_input = pick_back(arrived_head, arrived.reshape(pair_count, -1)).reshape(
        head_count, box_side, box_side, channels
    )
    factor = 1.0 / math.sqrt(lax.axis_size("row") * columns * head_count * box_side * box_side)
    cotangent = head_cot[:, 0]
    pre_one = conv_pad(box_input, head_w1, 1)
    hidden = jax.nn.silu(pre_one).astype(jnp.bfloat16)
    pre_two = conv_pad(hidden, head_w2, 1)
    delta_two = (cotangent.astype(jnp.float32) * silu_slope(pre_two)).astype(jnp.bfloat16)
    second_local = weight_grad(hidden, delta_two)
    delta_one = (conv_pad(delta_two, flip_weights(head_w2), 1) * silu_slope(pre_one)).astype(
        jnp.bfloat16
    )
    box_grads = conv_pad(delta_one, flip_weights(head_w1), 1).astype(jnp.bfloat16)
    sent_back = pick_rows(arrived_head, box_grads).reshape(
        columns, capacity, box_side, box_side, channels
    )
    returned = lax.all_to_all(sent_back, "col", split_axis=0, concat_axis=0, tiled=True)
    slot_grads = pick_back(send_map, returned.reshape(pair_count, -1)).reshape(
        slot_count, box_side, box_side, channels
    )
    first_local = weight_grad(box_input, delta_one)
    first_sum, second_sum = lax.psum((first_local, second_local), ("row", "col"))

    def add_box(slot, running):
        current = lax.dynamic_slice(
            running, (top_row[slot], left_col[slot], zero_index), (box_side, box_side, channels)
        )
        return lax.dynamic_update_slice(
            running,
            current + slot_grads[slot].astype(jnp.float32),
            (top_row[slot], left_col[slot], zero_index),
        )

    box_total = lax.fori_loop(
        0, slot_count, add_box, jnp.zeros((tile_rows, tile_cols, channels), jnp.float32)
    )
    delta_map = (box_total * silu_slope(preact)).astype(jnp.bfloat16)
    delta_rim = padded_2(delta_map, (("row", 0), ("col", 1)), 1)
    grad_map = conv_pad(delta_rim[None], flip_weights(tile_w), 0)[0].astype(jnp.bfloat16)
    return (grad_map, first_sum * factor, second_sum * factor)


def solution(mesh):
    in_specs = (
        P("row", "col", None),
        P(),
        P(),
        P(),
        P("row", "col"),
        P("row", "col"),
        P("row", "col"),
        P("row", "col", None, None, None),
    )
    out_specs = (P("row", "col", None), P(), P())
    return jax.shard_map(body, mesh=mesh, in_specs=in_specs, out_specs=out_specs, check_vma=False)
```

profile of v0, /device:TPU:98, one launch (start us, length us, event | category | flops | bytes accessed | tf_op | source)
XLA Modules:
  0.0 488.1 jit_solution(9538092367469643481)
XLA Ops:
  8.0 4.3 collective-permute-start.1
  12.3 1.9 collective-permute-start
  20.6 5.2 %collective-permute-start.2 = (bf16[18,1,256]{2,1,0:T(2,128)(2,1)S(1)}, bf16[18,1,256]{2,1,0:T(2,128)(2,1)S(1)}, u32[]{:S(2)}, u32[]{:S(2)}) collective-permute-start(bf16[18,1,256]{2,1,0:T(2,128)(2,1)S(1)} %get-tuple-element.157), channel_id=1, source_target_pairs={{0,1},{1,2},{2,3},{3,4},{4,5},{5,6},{6,7},{8,9},{9,10},{10,11},{11... | collective-permute-start | bytes 27656 | tf_op jit(solution)/shard_map/ppermute | solution.py:17
  25.7 1.9 collective-permute-start.3
  27.7 4.9 %collective-permute-done.3 = bf16[18,1,256]{2,1,0:T(2,128)(2,1)S(1)} collective-permute-done((bf16[18,1,256]{2,1,0:T(2,128)(2,1)S(1)}, bf16[18,1,256]{2,1,0:T(2,128)(2,1)S(1)}, u32[]{:S(2)}, u32[]{:S(2)}) %collective-permute-start.3) | collective-permute-done | bytes 9248 | tf_op jit(solution)/shard_map/ppermute | solution.py:18
  35.2 41.9 %while.15 = (s32[]{:T(128)}, bf16[16,32,256]{2,0,1:T(8,128)(2,1)S(1)}, s32[16,3]{0,1:T(4,128)S(1)}, bf16[16,14,14,256]{3,2,1,0:T(8,128)(2,1)}, s32[]{:T(128)}) while((s32[]{:T(128)}, bf16[16,32,256]{2,0,1:T(8,128)(2,1)S(1)}, s32[16,3]{0,1:T(4,128)S(1)}, bf16[16,14,14,256]{3,2,1,0:T(8,128)(2,1)}, s32[]{:T(128)}) %tuple.61), condition=%wide.while_cond, body=%wide.while_body.sunk | while | flops 2 | bytes 415869 | solution.py:105
  77.2 2.4 reshape.125
  81.3 2.6 reshape.126
  83.9 3.6 copy.100
  87.6 5.2 %all-to-all-start.1 = ((bf16[8,2,14,14,256]{4,1,3,2,0:T(2,128)(2,1)}), bf16[8,2,14,14,256]{4,1,3,2,0:T(2,128)(2,1)}, u32[]{:S(2)}, u32[]{:S(2)}) async-start(bf16[8,2,14,14,256]{4,1,3,2,0:T(2,128)(2,1)} %copy.100), calls=%async_computation.1 | async-start | bytes 3211264 | tf_op jit(solution)/shard_map/all_to_all | solution.py:109
  93.8 32.7 %all-to-all-done.1 = bf16[8,2,14,14,256]{4,1,3,2,0:T(2,128)(2,1)} async-done(((bf16[8,2,14,14,256]{4,1,3,2,0:T(2,128)(2,1)}), bf16[8,2,14,14,256]{4,1,3,2,0:T(2,128)(2,1)}, u32[]{:S(2)}, u32[]{:S(2)}) %all-to-all-start.1) | async-done | bytes 1605664 | tf_op jit(solution)/shard_map/all_to_all | solution.py:109
  126.4 6.7 %all-to-all-start = ((bf16[8,2,4]{2,1,0:T(2,128)(2,1)}), bf16[8,2,4]{2,1,0:T(2,128)(2,1)S(1)}, u32[]{:S(2)}, u32[]{:S(2)}) async-start(bf16[8,2,4]{2,1,0:T(2,128)(2,1)} %bitcast.9), calls=%async_computation | async-start | bytes 8192 | tf_op jit(solution)/shard_map/all_to_all | solution.py:110
  134.8 2.1 reshape.127
  160.7 3.7 copy.109
  164.4 6.9 %all-to-all-start.2 = ((bf16[8,2,14,14,256]{4,1,3,2,0:T(2,128)(2,1)}), bf16[8,2,14,14,256]{4,1,3,2,0:T(2,128)(2,1)S(1)}, u32[]{:S(2)}, u32[]{:S(2)}) async-start(bf16[8,2,14,14,256]{4,1,3,2,0:T(2,128)(2,1)} %copy.109), calls=%async_computation.2 | async-start | bytes 3211264 | tf_op jit(solution)/shard_map/all_to_all | solution.py:130
  189.3 15.8 %all-to-all-done.2 = bf16[8,2,14,14,256]{4,1,3,2,0:T(2,128)(2,1)S(1)} async-done(((bf16[8,2,14,14,256]{4,1,3,2,0:T(2,128)(2,1)}), bf16[8,2,14,14,256]{4,1,3,2,0:T(2,128)(2,1)S(1)}, u32[]{:S(2)}, u32[]{:S(2)}) %all-to-all-start.2) | async-done | bytes 1605664 | tf_op jit(solution)/shard_map/all_to_all | solution.py:130
  208.9 90.9 %while.14 = (s32[]{:T(128)}, f32[16,32,256]{2,0,1:T(8,128)S(1)}, s32[16]{0:T(128)S(1)}, s32[16]{0:T(128)S(1)}, bf16[16,14,14,256]{3,2,1,0:T(8,128)(2,1)S(1)}, /*index=5*/s32[]{:T(128)}, s32[]{:T(128)}, s32[]{:T(128)}, s32[]{:T(128)}) while((s32[]{:T(128)}, f32[16,32,256]{2,0,1:T(8,128)S(1)}, s32[16]{0:T(128)S(1)}, s32[16]{0:T(128)S(1)}, ...), condition=%wide.region_2.3_spmd, body=%wide.region_1.2_spmd.sunk | while | flops 100360 | bytes 1706193 | solution.py:147
  300.1 1.9 collective-permute-start.4
  302.0 5.8 %collective-permute-start.5 = (bf16[1,32,256]{2,0,1:T(2,128)(2,1)S(1)}, bf16[1,32,256]{2,0,1:T(2,128)(2,1)S(1)}, u32[]{:S(2)}, u32[]{:S(2)}) collective-permute-start(bf16[1,32,256]{2,0,1:T(2,128)(2,1)S(1)} %get-tuple-element.160), channel_id=1, source_target_pairs={{8,0},{16,8},{24,16},{32,24},{40,32},{48,40},{56,48},{64,56},{72,6... | collective-permute-start | bytes 49160 | tf_op jit(solution)/shard_map/ppermute | solution.py:18
  307.8 155.4 %all-reduce.5.cloned.1.call-done = (f32[3,3,256,256]{3,2,1,0:T(8,128)}, f32[3,3,256,256]{3,2,1,0:T(8,128)}) async-done(((f32[3,3,256,256]{3,2,1,0:T(8,128)}, f32[3,3,256,256]{3,2,1,0:T(8,128)}), (f32[3,3,256,256]{3,2,1,0:T(8,128)}, f32[3,3,256,256]{3,2,1,0:T(8,128)})) %all-reduce.5.cloned.1.call-update) | async-done | bytes 4718608 | tf_op jit(solution)/shard_map/psum | solution.py:135
  463.2 3.4 broadcast_multiply_fusion.1
  466.7 5.5 %collective-permute-start.6 = (bf16[18,1,256]{2,0,1:T(8,128)(2,1)S(1)}, bf16[18,1,256]{2,0,1:T(8,128)(2,1)S(1)}, u32[]{:S(2)}, u32[]{:S(2)}) collective-permute-start(bf16[18,1,256]{2,0,1:T(8,128)(2,1)S(1)} %get-tuple-element.155), channel_id=1, source_target_pairs={{0,1},{1,2},{2,3},{3,4},{4,5},{5,6},{6,7},{8,9},{9,10},{10,11},{11... | collective-permute-start | bytes 27656 | tf_op jit(solution)/shard_map/ppermute | solution.py:17
  472.1 1.9 collective-permute-start.7
  475.7 3.2 collective-permute-done.7
  (319 shorter events, 133.2 us)
Async XLA Ops:
  7.2 137.5 %copy-start = (bf16[3,3,256,256]{3,2,1,0:T(8,128)(2,1)S(1)}, bf16[3,3,256,256]{3,2,1,0:T(8,128)(2,1)}, u32[]{:S(2)}) copy-start(bf16[3,3,256,256]{3,2,1,0:T(8,128)(2,1)} %param.13) | copy-start | bytes 3538948
  8.0 12.5 %collective-permute-start.1 = (bf16[1,32,256]{2,1,0:T(8,128)(2,1)S(1)}, bf16[1,32,256]{2,1,0:T(8,128)(2,1)S(1)}, u32[]{:S(2)}, u32[]{:S(2)}) collective-permute-start(bf16[1,32,256]{2,1,0:T(8,128)(2,1)S(1)} %get-tuple-element.161), channel_id=1, source_target_pairs={{8,0},{16,8},{24,16},{32,24},{40,32},{48,40},{56,48},{64,56},{72,6... | collective-permute-start | bytes 49160 | tf_op jit(solution)/shard_map/ppermute | solution.py:18
  12.3 7.2 %collective-permute-start = (bf16[1,32,256]{2,1,0:T(8,128)(2,1)S(1)}, bf16[1,32,256]{2,1,0:T(8,128)(2,1)S(1)}, u32[]{:S(2)}, u32[]{:S(2)}) collective-permute-start(bf16[1,32,256]{2,1,0:T(8,128)(2,1)S(1)} %get-tuple-element.162), channel_id=1, source_target_pairs={{0,8},{8,16},{16,24},{24,32},{32,40},{40,48},{48,56},{56,64},{64,7... | collective-permute-start | bytes 49160 | tf_op jit(solution)/shard_map/ppermute | solution.py:17
  20.5 12.6 %copy-start.22 = (bf16[3,3,256,256]{3,2,1,0:T(8,128)(2,1)S(1)}, bf16[3,3,256,256]{3,2,1,0:T(8,128)(2,1)}, u32[]{:S(2)}) copy-start(bf16[3,3,256,256]{3,2,1,0:T(8,128)(2,1)} %param.11) | copy-start | bytes 3538948
  20.5 12.6 %copy-start.25 = (pred[8,5]{0,1:T(8,128)(4,1)S(1)}, pred[8,5]{0,1:T(8,128)(4,1)}, u32[]{:S(2)}) copy-start(pred[8,5]{0,1:T(8,128)(4,1)} %constant.124) | copy-start | bytes 124
  20.6 7.1 %collective-permute-start.2 = (bf16[18,1,256]{2,1,0:T(2,128)(2,1)S(1)}, bf16[18,1,256]{2,1,0:T(2,128)(2,1)S(1)}, u32[]{:S(2)}, u32[]{:S(2)}) collective-permute-start(bf16[18,1,256]{2,1,0:T(2,128)(2,1)S(1)} %get-tuple-element.157), channel_id=1, source_target_pairs={{0,1},{1,2},{2,3},{3,4},{4,5},{5,6},{6,7},{8,9},{9,10},{10,11},{11... | collective-permute-start | bytes 27656 | tf_op jit(solution)/shard_map/ppermute | solution.py:17
  25.7 6.9 %collective-permute-start.3 = (bf16[18,1,256]{2,1,0:T(2,128)(2,1)S(1)}, bf16[18,1,256]{2,1,0:T(2,128)(2,1)S(1)}, u32[]{:S(2)}, u32[]{:S(2)}) collective-permute-start(bf16[18,1,256]{2,1,0:T(2,128)(2,1)S(1)} %get-tuple-element.158), channel_id=1, source_target_pairs={{1,0},{2,1},{3,2},{4,3},{5,4},{6,5},{7,6},{9,8},{10,9},{11,10},{12... | collective-permute-start | bytes 27656 | tf_op jit(solution)/shard_map/ppermute | solution.py:18
  87.6 5.2 %copy-start.24 = (s32[16,1]{0,1:T(1,128)S(1)}, s32[16,1]{0,1:T(1,128)}, u32[]{:S(2)}) copy-start(s32[16,1]{0,1:T(1,128)} %param.16) | copy-start | bytes 196
  87.6 38.8 %all-to-all-start.1 = ((bf16[8,2,14,14,256]{4,1,3,2,0:T(2,128)(2,1)}), bf16[8,2,14,14,256]{4,1,3,2,0:T(2,128)(2,1)}, u32[]{:S(2)}, u32[]{:S(2)}) async-start(bf16[8,2,14,14,256]{4,1,3,2,0:T(2,128)(2,1)} %copy.100), calls=%async_computation.1 | async-start | bytes 3211264 | tf_op jit(solution)/shard_map/all_to_all | solution.py:109
  126.4 11.1 %all-to-all-start = ((bf16[8,2,4]{2,1,0:T(2,128)(2,1)}), bf16[8,2,4]{2,1,0:T(2,128)(2,1)S(1)}, u32[]{:S(2)}, u32[]{:S(2)}) async-start(bf16[8,2,4]{2,1,0:T(2,128)(2,1)} %bitcast.9), calls=%async_computation | async-start | bytes 8192 | tf_op jit(solution)/shard_map/all_to_all | solution.py:110
  140.6 12.0 %copy-start.8 = (bf16[4,14,14,256]{3,2,1,0:T(8,128)(2,1)}, bf16[4,14,14,256]{3,2,1,0:T(8,128)(2,1)S(1)}, u32[]{:S(2)}) copy-start(bf16[4,14,14,256]{3,2,1,0:T(8,128)(2,1)S(1)} %reshape.128) | copy-start | bytes 1204228
  153.7 2.4 copy-start.21
  164.4 6.9 %copy-start.7 = (bf16[14,4,16,256]{3,2,1,0:T(8,128)(2,1)S(1)}, bf16[14,4,16,256]{3,2,1,0:T(8,128)(2,1)}, u32[]{:S(2)}) copy-start(bf16[14,4,16,256]{3,2,1,0:T(8,128)(2,1)} %copy-done.6) | copy-start | bytes 1376260
  164.4 6.9 %copy-start.9 = (bf16[4,14,14,256]{3,2,1,0:T(8,128)(2,1)S(1)}, bf16[4,14,14,256]{3,2,1,0:T(8,128)(2,1)}, u32[]{:S(2)}) copy-start(bf16[4,14,14,256]{3,2,1,0:T(8,128)(2,1)} %copy-done.8) | copy-start | bytes 1204228
  164.4 40.7 %all-to-all-start.2 = ((bf16[8,2,14,14,256]{4,1,3,2,0:T(2,128)(2,1)}), bf16[8,2,14,14,256]{4,1,3,2,0:T(2,128)(2,1)S(1)}, u32[]{:S(2)}, u32[]{:S(2)}) async-start(bf16[8,2,14,14,256]{4,1,3,2,0:T(2,128)(2,1)} %copy.109), calls=%async_computation.2 | async-start | bytes 3211264 | tf_op jit(solution)/shard_map/all_to_all | solution.py:130
  171.3 291.9 %all-reduce.5.cloned.1.call-start = ((), (), s32[]{:S(2)}) async-start(), calls=%async_computation.3 | async-start | bytes 9437184 | tf_op jit(solution)/shard_map/psum | solution.py:135
  208.9 90.9 %copy-start.3 = (f32[16,8,5,256]{3,0,2,1:T(8,128)S(1)}, f32[16,8,5,256]{3,0,2,1:T(8,128)}, u32[]{:S(2)}) copy-start(f32[16,8,5,256]{3,0,2,1:T(8,128)} %copy-done.2) | copy-start | bytes 1966084
  300.1 166.5 %collective-permute-start.4 = (bf16[1,32,256]{2,0,1:T(2,128)(2,1)S(1)}, bf16[1,32,256]{2,0,1:T(2,128)(2,1)S(1)}, u32[]{:S(2)}, u32[]{:S(2)}) collective-permute-start(bf16[1,32,256]{2,0,1:T(2,128)(2,1)S(1)} %get-tuple-element.159), channel_id=1, source_target_pairs={{0,8},{8,16},{16,24},{24,32},{32,40},{40,48},{48,56},{56,64},{64,7... | collective-permute-start | bytes 49160 | tf_op jit(solution)/shard_map/ppermute | solution.py:17
  302.0 164.6 %collective-permute-start.5 = (bf16[1,32,256]{2,0,1:T(2,128)(2,1)S(1)}, bf16[1,32,256]{2,0,1:T(2,128)(2,1)S(1)}, u32[]{:S(2)}, u32[]{:S(2)}) collective-permute-start(bf16[1,32,256]{2,0,1:T(2,128)(2,1)S(1)} %get-tuple-element.160), channel_id=1, source_target_pairs={{8,0},{16,8},{24,16},{32,24},{40,32},{48,40},{56,48},{64,56},{72,6... | collective-permute-start | bytes 49160 | tf_op jit(solution)/shard_map/ppermute | solution.py:18
  463.2 10.9 %copy-start.4 = (f32[3,3,256,256]{3,2,1,0:T(8,128)S(1)}, f32[3,3,256,256]{3,2,1,0:T(8,128)}, u32[]{:S(2)}) copy-start(f32[3,3,256,256]{3,2,1,0:T(8,128)} %get-tuple-element.146) | copy-start | bytes 7077892
  466.7 9.0 %collective-permute-start.6 = (bf16[18,1,256]{2,0,1:T(8,128)(2,1)S(1)}, bf16[18,1,256]{2,0,1:T(8,128)(2,1)S(1)}, u32[]{:S(2)}, u32[]{:S(2)}) collective-permute-start(bf16[18,1,256]{2,0,1:T(8,128)(2,1)S(1)} %get-tuple-element.155), channel_id=1, source_target_pairs={{0,1},{1,2},{2,3},{3,4},{4,5},{5,6},{6,7},{8,9},{9,10},{10,11},{11... | collective-permute-start | bytes 27656 | tf_op jit(solution)/shard_map/ppermute | solution.py:17
  472.1 6.8 %collective-permute-start.7 = (bf16[18,1,256]{2,0,1:T(8,128)(2,1)S(1)}, bf16[18,1,256]{2,0,1:T(8,128)(2,1)S(1)}, u32[]{:S(2)}, u32[]{:S(2)}) collective-permute-start(bf16[18,1,256]{2,0,1:T(8,128)(2,1)S(1)} %get-tuple-element.156), channel_id=1, source_target_pairs={{1,0},{2,1},{3,2},{4,3},{5,4},{6,5},{7,6},{9,8},{10,9},{11,10},{12... | collective-permute-start | bytes 27656 | tf_op jit(solution)/shard_map/ppermute | solution.py:18
  475.7 3.7 copy-start.23
  479.4 1.9 copy-start.1
  (14 other events, 15.8 us)
Sparse Core Ops, SparseCore 0:
  189.4 273.7 all-reduce.4
where the time goes:
time: 491 us; the launch traced here: 488 us
  waiting for transfers between devices  214 us (44%)
  local copies, waits for them, and re-layouts  104 us (21%)
  loops' own time  63.1 us (13%)
  starting transfers between devices  47.2 us (10%)
  matrix products  30.9 us (6%)
  between operations  14.8 us (3%)
  other arithmetic  13.8 us (3%)
    psum x1, waiting for transfers between devices, body(): lax.psum((first_local, second_local), ('row', 'col'))  155 us
    another operation x1, loops' own time, body(): lax.fori_loop(0, slot_count, add_box, jnp.zeros((tile_rows, tile_cols, ch...  62.9 us
    gather x64, local copies, waits for them, and re-layouts  41.8 us
    all_to_all x1, waiting for transfers between devices, body(): lax.all_to_all(outgoing, 'col', split_axis=0, concat_axis=0, tiled=True)  32.7 us
    dot_general x18, matrix products, weight_grad(): lax.dot_general(window, flat_delta, (((0,), (0,)), ((), ())), preferred_e...  18.9 us
    all_to_all x1, waiting for transfers between devices, body(): lax.all_to_all(sent_back, 'col', split_axis=0, concat_axis=0, tiled=True)  15.8 us
    ppermute x4, starting transfers between devices, padded_2(): before = lax.ppermute(last, axis, up)  14.5 us
    ppermute x4, starting transfers between devices, padded_2(): after = lax.ppermute(leading, axis, down)  13.9 us
  transfers between devices with their start and end apart: 12, of which 7 were waited for; matrix products, arithmetic and copies ran while one was open for 13% of the time, Pallas kernels for 0%

commit v1 on v0

--- a/solution.py
+++ b/solution.py
@@ -132,7 +132,7 @@
         slot_count, box_side, box_side, channels
     )
     first_local = weight_grad(box_input, delta_one)
-    first_sum, second_sum = lax.psum((first_local, second_local), ("row", "col"))
+    first_sum, second_sum = lax.psum(lax.psum((first_local, second_local), "row"), "col")
 
     def add_box(slot, running):
         current = lax.dynamic_slice(

time: 491 us -> 453 us (0.923)
  waiting for transfers between devices: 214 us -> 175 us
    psum x1 -> x2, waiting for transfers between devices: 155 us -> 129 us  [the longest x1 125 us: body(): lax.psum((first_local, second_local), 'row')]
    all_to_all x1, waiting for transfers between devices: 15.8 us -> 0.01 us  [body(): lax.all_to_all(sent_back, 'col', split_axis=0, concat_axis=0, tiled=True)]
  transfers between devices with their start and end apart: 12 -> 13, of which waited for: 7 -> 8; matrix products, arithmetic and copies ran while one was open for 13% -> 14% of each run, Pallas kernels for 0% -> 0%
where the time goes in v1:
time: 453 us; the launch traced here: 448 us
  waiting for transfers between devices  175 us (39%)
  local copies, waits for them, and re-layouts  104 us (23%)
  loops' own time  63.1 us (14%)
  starting transfers between devices  46.5 us (10%)
  matrix products  30.9 us (7%)
  between operations  14.8 us (3%)
  other arithmetic  13.9 us (3%)
    psum x1, waiting for transfers between devices, body(): lax.psum((first_local, second_local), 'row')  125 us
    another operation x1, loops' own time, body(): lax.fori_loop(0, slot_count, add_box, jnp.zeros((tile_rows, tile_cols, ch...  62.9 us
    gather x64, local copies, waits for them, and re-layouts  41.3 us
    all_to_all x1, waiting for transfers between devices, body(): lax.all_to_all(outgoing, 'col', split_axis=0, concat_axis=0, tiled=True)  32.7 us
    dot_general x18, matrix products, weight_grad(): lax.dot_general(window, flat_delta, (((0,), (0,)), ((), ())), preferred_e...  18.9 us
    ppermute x4, starting transfers between devices, padded_2(): before = lax.ppermute(last, axis, up)  13.9 us
    ppermute x4, starting transfers between devices, padded_2(): after = lax.ppermute(leading, axis, down)  13.8 us
    ppermute x4, waiting for transfers between devices, padded_2(): after = lax.ppermute(leading, axis, down)  11.5 us
  transfers between devices with their start and end apart: 13, of which 8 were waited for; matrix products, arithmetic and copies ran while one was open for 14% of the time, Pallas kernels for 0%

profile of v1, /device:TPU:98, one launch (start us, length us, event | category | flops | bytes accessed | tf_op | source)
XLA Modules:
  0.0 448.1 jit_solution(15442169880152659923)
XLA Ops:
  8.0 4.3 collective-permute-start.1
  12.3 1.9 collective-permute-start
  20.6 5.2 %collective-permute-start.2 = (bf16[18,1,256]{2,1,0:T(2,128)(2,1)S(1)}, bf16[18,1,256]{2,1,0:T(2,128)(2,1)S(1)}, u32[]{:S(2)}, u32[]{:S(2)}) collective-permute-start(bf16[18,1,256]{2,1,0:T(2,128)(2,1)S(1)} %get-tuple-element.159), channel_id=1, source_target_pairs={{0,1},{1,2},{2,3},{3,4},{4,5},{5,6},{6,7},{8,9},{9,10},{10,11},{11... | collective-permute-start | bytes 27656 | tf_op jit(solution)/shard_map/ppermute | solution.py:17
  25.7 1.9 collective-permute-start.3
  27.7 4.9 %collective-permute-done.3 = bf16[18,1,256]{2,1,0:T(2,128)(2,1)S(1)} collective-permute-done((bf16[18,1,256]{2,1,0:T(2,128)(2,1)S(1)}, bf16[18,1,256]{2,1,0:T(2,128)(2,1)S(1)}, u32[]{:S(2)}, u32[]{:S(2)}) %collective-permute-start.3) | collective-permute-done | bytes 9248 | tf_op jit(solution)/shard_map/ppermute | solution.py:18
  35.3 41.5 %while.15 = (s32[]{:T(128)}, bf16[16,32,256]{2,0,1:T(8,128)(2,1)S(1)}, s32[16,3]{0,1:T(4,128)S(1)}, bf16[16,14,14,256]{3,2,1,0:T(8,128)(2,1)}, s32[]{:T(128)}) while((s32[]{:T(128)}, bf16[16,32,256]{2,0,1:T(8,128)(2,1)S(1)}, s32[16,3]{0,1:T(4,128)S(1)}, bf16[16,14,14,256]{3,2,1,0:T(8,128)(2,1)}, s32[]{:T(128)}) %tuple.61), condition=%wide.while_cond, body=%wide.while_body.sunk | while | flops 2 | bytes 415869 | solution.py:105
  76.8 2.4 reshape.125
  80.9 2.6 reshape.126
  83.5 3.6 copy.100
  87.2 5.2 %all-to-all-start.1 = ((bf16[8,2,14,14,256]{4,1,3,2,0:T(2,128)(2,1)}), bf16[8,2,14,14,256]{4,1,3,2,0:T(2,128)(2,1)}, u32[]{:S(2)}, u32[]{:S(2)}) async-start(bf16[8,2,14,14,256]{4,1,3,2,0:T(2,128)(2,1)} %copy.100), calls=%async_computation.1 | async-start | bytes 3211264 | tf_op jit(solution)/shard_map/all_to_all | solution.py:109
  93.4 32.7 %all-to-all-done.1 = bf16[8,2,14,14,256]{4,1,3,2,0:T(2,128)(2,1)} async-done(((bf16[8,2,14,14,256]{4,1,3,2,0:T(2,128)(2,1)}), bf16[8,2,14,14,256]{4,1,3,2,0:T(2,128)(2,1)}, u32[]{:S(2)}, u32[]{:S(2)}) %all-to-all-start.1) | async-done | bytes 1605664 | tf_op jit(solution)/shard_map/all_to_all | solution.py:109
  126.0 6.7 %all-to-all-start = ((bf16[8,2,4]{2,1,0:T(2,128)(2,1)}), bf16[8,2,4]{2,1,0:T(2,128)(2,1)S(1)}, u32[]{:S(2)}, u32[]{:S(2)}) async-start(bf16[8,2,4]{2,1,0:T(2,128)(2,1)} %bitcast.9), calls=%async_computation | async-start | bytes 8192 | tf_op jit(solution)/shard_map/all_to_all | solution.py:110
  134.4 2.1 reshape.127
  160.4 3.7 copy.109
  164.1 6.9 %all-to-all-start.2 = ((bf16[8,2,14,14,256]{4,1,3,2,0:T(2,128)(2,1)}), bf16[8,2,14,14,256]{4,1,3,2,0:T(2,128)(2,1)S(1)}, u32[]{:S(2)}, u32[]{:S(2)}) async-start(bf16[8,2,14,14,256]{4,1,3,2,0:T(2,128)(2,1)} %copy.109), calls=%async_computation.2 | async-start | bytes 3211264 | tf_op jit(solution)/shard_map/all_to_all | solution.py:130
  189.1 125.2 %all-reduce.7.cloned.1.call-done = (f32[3,3,256,256]{3,2,1,0:T(8,128)}, f32[3,3,256,256]{3,2,1,0:T(8,128)}) async-done(((f32[3,3,256,256]{3,2,1,0:T(8,128)}, f32[3,3,256,256]{3,2,1,0:T(8,128)}), (f32[3,3,256,256]{3,2,1,0:T(8,128)}, f32[3,3,256,256]{3,2,1,0:T(8,128)})) %all-reduce.7.cloned.1.call-update) | async-done | bytes 4718608 | tf_op jit(solution)/shard_map/psum | solution.py:135
  318.1 90.9 %while.14 = (s32[]{:T(128)}, f32[16,32,256]{2,0,1:T(8,128)S(1)}, s32[16]{0:T(128)S(1)}, s32[16]{0:T(128)S(1)}, bf16[16,14,14,256]{3,2,1,0:T(8,128)(2,1)S(1)}, /*index=5*/s32[]{:T(128)}, s32[]{:T(128)}, s32[]{:T(128)}, s32[]{:T(128)}) while((s32[]{:T(128)}, f32[16,32,256]{2,0,1:T(8,128)S(1)}, s32[16]{0:T(128)S(1)}, s32[16]{0:T(128)S(1)}, ...), condition=%wide.region_2.3_spmd, body=%wide.region_1.2_spmd.sunk | while | flops 100360 | bytes 1706193 | solution.py:147
  409.3 2.2 collective-permute-start.4
  411.5 5.6 %collective-permute-start.5 = (bf16[1,32,256]{2,0,1:T(2,128)(2,1)S(1)}, bf16[1,32,256]{2,0,1:T(2,128)(2,1)S(1)}, u32[]{:S(2)}, u32[]{:S(2)}) collective-permute-start(bf16[1,32,256]{2,0,1:T(2,128)(2,1)S(1)} %get-tuple-element.162), channel_id=1, source_target_pairs={{8,0},{16,8},{24,16},{32,24},{40,32},{48,40},{56,48},{64,56},{72,6... | collective-permute-start | bytes 49160 | tf_op jit(solution)/shard_map/ppermute | solution.py:18
  418.7 4.6 %collective-permute-start.6 = (bf16[18,1,256]{2,0,1:T(8,128)(2,1)S(1)}, bf16[18,1,256]{2,0,1:T(8,128)(2,1)S(1)}, u32[]{:S(2)}, u32[]{:S(2)}) collective-permute-start(bf16[18,1,256]{2,0,1:T(8,128)(2,1)S(1)} %get-tuple-element.157), channel_id=1, source_target_pairs={{0,1},{1,2},{2,3},{3,4},{4,5},{5,6},{6,7},{8,9},{9,10},{10,11},{11... | collective-permute-start | bytes 27656 | tf_op jit(solution)/shard_map/ppermute | solution.py:17
  423.3 1.9 collective-permute-start.7
  425.3 5.1 %collective-permute-done.7 = bf16[18,1,256]{2,0,1:T(8,128)(2,1)S(1)} collective-permute-done((bf16[18,1,256]{2,0,1:T(8,128)(2,1)S(1)}, bf16[18,1,256]{2,0,1:T(8,128)(2,1)S(1)}, u32[]{:S(2)}, u32[]{:S(2)}) %collective-permute-start.7) | collective-permute-done | bytes 9248 | tf_op jit(solution)/shard_map/ppermute | solution.py:18
  432.7 3.5 all-reduce.9.cloned.1.call-done
  436.2 3.4 broadcast_multiply_fusion.1
  (326 shorter events, 134.5 us)
Async XLA Ops:
  7.2 137.1 %copy-start = (bf16[3,3,256,256]{3,2,1,0:T(8,128)(2,1)S(1)}, bf16[3,3,256,256]{3,2,1,0:T(8,128)(2,1)}, u32[]{:S(2)}) copy-start(bf16[3,3,256,256]{3,2,1,0:T(8,128)(2,1)} %param.13) | copy-start | bytes 3538948
  8.0 12.5 %collective-permute-start.1 = (bf16[1,32,256]{2,1,0:T(8,128)(2,1)S(1)}, bf16[1,32,256]{2,1,0:T(8,128)(2,1)S(1)}, u32[]{:S(2)}, u32[]{:S(2)}) collective-permute-start(bf16[1,32,256]{2,1,0:T(8,128)(2,1)S(1)} %get-tuple-element.163), channel_id=1, source_target_pairs={{8,0},{16,8},{24,16},{32,24},{40,32},{48,40},{56,48},{64,56},{72,6... | collective-permute-start | bytes 49160 | tf_op jit(solution)/shard_map/ppermute | solution.py:18
  12.3 7.2 %collective-permute-start = (bf16[1,32,256]{2,1,0:T(8,128)(2,1)S(1)}, bf16[1,32,256]{2,1,0:T(8,128)(2,1)S(1)}, u32[]{:S(2)}, u32[]{:S(2)}) collective-permute-start(bf16[1,32,256]{2,1,0:T(8,128)(2,1)S(1)} %get-tuple-element.164), channel_id=1, source_target_pairs={{0,8},{8,16},{16,24},{24,32},{32,40},{40,48},{48,56},{56,64},{64,7... | collective-permute-start | bytes 49160 | tf_op jit(solution)/shard_map/ppermute | solution.py:17
  20.5 12.6 %copy-start.24 = (bf16[3,3,256,256]{3,2,1,0:T(8,128)(2,1)S(1)}, bf16[3,3,256,256]{3,2,1,0:T(8,128)(2,1)}, u32[]{:S(2)}) copy-start(bf16[3,3,256,256]{3,2,1,0:T(8,128)(2,1)} %param.11) | copy-start | bytes 3538948
  20.5 12.6 %copy-start.27 = (pred[8,5]{0,1:T(8,128)(4,1)S(1)}, pred[8,5]{0,1:T(8,128)(4,1)}, u32[]{:S(2)}) copy-start(pred[8,5]{0,1:T(8,128)(4,1)} %constant.124) | copy-start | bytes 124
  20.6 7.1 %collective-permute-start.2 = (bf16[18,1,256]{2,1,0:T(2,128)(2,1)S(1)}, bf16[18,1,256]{2,1,0:T(2,128)(2,1)S(1)}, u32[]{:S(2)}, u32[]{:S(2)}) collective-permute-start(bf16[18,1,256]{2,1,0:T(2,128)(2,1)S(1)} %get-tuple-element.159), channel_id=1, source_target_pairs={{0,1},{1,2},{2,3},{3,4},{4,5},{5,6},{6,7},{8,9},{9,10},{10,11},{11... | collective-permute-start | bytes 27656 | tf_op jit(solution)/shard_map/ppermute | solution.py:17
  25.7 6.9 %collective-permute-start.3 = (bf16[18,1,256]{2,1,0:T(2,128)(2,1)S(1)}, bf16[18,1,256]{2,1,0:T(2,128)(2,1)S(1)}, u32[]{:S(2)}, u32[]{:S(2)}) collective-permute-start(bf16[18,1,256]{2,1,0:T(2,128)(2,1)S(1)} %get-tuple-element.160), channel_id=1, source_target_pairs={{1,0},{2,1},{3,2},{4,3},{5,4},{6,5},{7,6},{9,8},{10,9},{11,10},{12... | collective-permute-start | bytes 27656 | tf_op jit(solution)/shard_map/ppermute | solution.py:18
  87.2 5.2 %copy-start.26 = (s32[16,1]{0,1:T(1,128)S(1)}, s32[16,1]{0,1:T(1,128)}, u32[]{:S(2)}) copy-start(s32[16,1]{0,1:T(1,128)} %param.16) | copy-start | bytes 196
  87.2 38.8 %all-to-all-start.1 = ((bf16[8,2,14,14,256]{4,1,3,2,0:T(2,128)(2,1)}), bf16[8,2,14,14,256]{4,1,3,2,0:T(2,128)(2,1)}, u32[]{:S(2)}, u32[]{:S(2)}) async-start(bf16[8,2,14,14,256]{4,1,3,2,0:T(2,128)(2,1)} %copy.100), calls=%async_computation.1 | async-start | bytes 3211264 | tf_op jit(solution)/shard_map/all_to_all | solution.py:109
  126.0 11.1 %all-to-all-start = ((bf16[8,2,4]{2,1,0:T(2,128)(2,1)}), bf16[8,2,4]{2,1,0:T(2,128)(2,1)S(1)}, u32[]{:S(2)}, u32[]{:S(2)}) async-start(bf16[8,2,4]{2,1,0:T(2,128)(2,1)} %bitcast.9), calls=%async_computation | async-start | bytes 8192 | tf_op jit(solution)/shard_map/all_to_all | solution.py:110
  140.2 12.0 %copy-start.9 = (bf16[4,14,14,256]{3,2,1,0:T(8,128)(2,1)}, bf16[4,14,14,256]{3,2,1,0:T(8,128)(2,1)S(1)}, u32[]{:S(2)}) copy-start(bf16[4,14,14,256]{3,2,1,0:T(8,128)(2,1)S(1)} %reshape.128) | copy-start | bytes 1204228
  154.1 3.0 copy-start.5
  164.1 6.9 %copy-start.8 = (bf16[14,4,16,256]{3,2,1,0:T(8,128)(2,1)S(1)}, bf16[14,4,16,256]{3,2,1,0:T(8,128)(2,1)}, u32[]{:S(2)}) copy-start(bf16[14,4,16,256]{3,2,1,0:T(8,128)(2,1)} %copy-done.7) | copy-start | bytes 1376260
  164.1 6.9 %copy-start.10 = (bf16[4,14,14,256]{3,2,1,0:T(8,128)(2,1)S(1)}, bf16[4,14,14,256]{3,2,1,0:T(8,128)(2,1)}, u32[]{:S(2)}) copy-start(bf16[4,14,14,256]{3,2,1,0:T(8,128)(2,1)} %copy-done.9) | copy-start | bytes 1204228
  164.1 150.2 %all-to-all-start.2 = ((bf16[8,2,14,14,256]{4,1,3,2,0:T(2,128)(2,1)}), bf16[8,2,14,14,256]{4,1,3,2,0:T(2,128)(2,1)S(1)}, u32[]{:S(2)}, u32[]{:S(2)}) async-start(bf16[8,2,14,14,256]{4,1,3,2,0:T(2,128)(2,1)} %copy.109), calls=%async_computation.2 | async-start | bytes 3211264 | tf_op jit(solution)/shard_map/all_to_all | solution.py:130
  171.0 143.3 %all-reduce.7.cloned.1.call-start = ((), (), s32[]{:S(2)}) async-start(), calls=%async_computation.3 | async-start | bytes 9437184 | tf_op jit(solution)/shard_map/psum | solution.py:135
  189.0 247.2 %all-reduce.9.cloned.1.call-start = ((), (), s32[]{:S(2)}) async-start(), calls=%async_computation.4 | async-start | bytes 9437184 | tf_op jit(solution)/shard_map/psum | solution.py:135
  318.1 90.9 %copy-start.3 = (f32[16,8,5,256]{3,0,2,1:T(8,128)S(1)}, f32[16,8,5,256]{3,0,2,1:T(8,128)}, u32[]{:S(2)}) copy-start(f32[16,8,5,256]{3,0,2,1:T(8,128)} %copy-done.2) | copy-start | bytes 1966084
  409.2 21.6 %copy-start.25 = (bf16[3,3,256,256]{3,2,1,0:T(8,128)(2,1)S(1)}, bf16[3,3,256,256]{3,2,1,0:T(8,128)(2,1)}, u32[]{:S(2)}) copy-start(bf16[3,3,256,256]{3,2,1,0:T(8,128)(2,1)} %param.11) | copy-start | bytes 3538948
  409.3 7.8 %collective-permute-start.4 = (bf16[1,32,256]{2,0,1:T(2,128)(2,1)S(1)}, bf16[1,32,256]{2,0,1:T(2,128)(2,1)S(1)}, u32[]{:S(2)}, u32[]{:S(2)}) collective-permute-start(bf16[1,32,256]{2,0,1:T(2,128)(2,1)S(1)} %get-tuple-element.161), channel_id=1, source_target_pairs={{0,8},{8,16},{16,24},{24,32},{32,40},{40,48},{48,56},{56,64},{64,7... | collective-permute-start | bytes 49160 | tf_op jit(solution)/shard_map/ppermute | solution.py:17
  411.5 7.2 %collective-permute-start.5 = (bf16[1,32,256]{2,0,1:T(2,128)(2,1)S(1)}, bf16[1,32,256]{2,0,1:T(2,128)(2,1)S(1)}, u32[]{:S(2)}, u32[]{:S(2)}) collective-permute-start(bf16[1,32,256]{2,0,1:T(2,128)(2,1)S(1)} %get-tuple-element.162), channel_id=1, source_target_pairs={{8,0},{16,8},{24,16},{32,24},{40,32},{48,40},{56,48},{64,56},{72,6... | collective-permute-start | bytes 49160 | tf_op jit(solution)/shard_map/ppermute | solution.py:18
  418.7 6.6 %collective-permute-start.6 = (bf16[18,1,256]{2,0,1:T(8,128)(2,1)S(1)}, bf16[18,1,256]{2,0,1:T(8,128)(2,1)S(1)}, u32[]{:S(2)}, u32[]{:S(2)}) collective-permute-start(bf16[18,1,256]{2,0,1:T(8,128)(2,1)S(1)} %get-tuple-element.157), channel_id=1, source_target_pairs={{0,1},{1,2},{2,3},{3,4},{4,5},{5,6},{6,7},{8,9},{9,10},{10,11},{11... | collective-permute-start | bytes 27656 | tf_op jit(solution)/shard_map/ppermute | solution.py:17
  423.3 7.0 %collective-permute-start.7 = (bf16[18,1,256]{2,0,1:T(8,128)(2,1)S(1)}, bf16[18,1,256]{2,0,1:T(8,128)(2,1)S(1)}, u32[]{:S(2)}, u32[]{:S(2)}) collective-permute-start(bf16[18,1,256]{2,0,1:T(8,128)(2,1)S(1)} %get-tuple-element.158), channel_id=1, source_target_pairs={{1,0},{2,1},{3,2},{4,3},{5,4},{6,5},{7,6},{9,8},{10,9},{11,10},{12... | collective-permute-start | bytes 27656 | tf_op jit(solution)/shard_map/ppermute | solution.py:18
  436.2 3.4 copy-start.4
  (17 other events, 20.5 us)
Sparse Core Ops, SparseCore 0:
  189.1 125.0 all-reduce.6
  316.8 119.3 all-reduce.8
